TPU v7x, 32 devices: a whole 2x2x4 slice. The times are simulated.
32 devices in a mesh: dp: 8 (over z, y), ctx: 4 (over x, core).
Axes of the slice: x: 2, y: 2, z: 4, core: 2. Of those that a mesh axis runs over, the one named last changes fastest.
Arguments:
- qkvu: bfloat16 [4096, 2048], P(('dp', 'ctx')), may hold values from -6 to 6
- actions: int32 [4096], P(('dp', 'ctx')), may hold values from 0 to 63
- lengths: int32 [8, 4], P('dp'), may hold values from 1 to 448, 512 in all within a row
- action_table: bfloat16 [64, 512], replicated, may hold values from -6 to 6
- gain: float32 [512], replicated, may hold values from 0.1 to 1.9
- w_out: bfloat16 [512, 1024], replicated, may hold values from -0.25 to 0.25
- cotangent: bfloat16 [4096, 1024], P(('dp', 'ctx')), may hold values from -6 to 6
Outputs:
- output: bfloat16 [4096, 1024], P(('dp', 'ctx'))
- d_qkvu: bfloat16 [4096, 2048], P(('dp', 'ctx'))
- d_wout: float32 [512, 1024], P('dp')
- d_table: float32 [64, 512], replicated
- d_gain: float32 [512], replicated
Inputs may be any that keep to these rules, and one draw needn't show every extreme that they name: Each row holds the lengths of the 4 histories packed in row order into one group's 512 rows; they sum to 512.
All inputs are finite; a program needn't handle non-finite values.
Results may differ from a plain program's by a relative error of at most 0.0066.
Values may be sent and summed in bfloat16 or wider, within the bound.
A program may use at most 64 MiB of HBM per device.

v0:
```python
import jax
import jax.numpy as jnp
from jax import lax
from jax.sharding import PartitionSpec as P

HD = 128
ACTIONS = 64


def silu_slope(inputs):
    sig = jax.nn.sigmoid(inputs)
    return sig * (1.0 + inputs * (1.0 - sig))


def history_of(positions, lengths_row):
    boundary = jnp.cumsum(lengths_row)
    history = jnp.sum((positions[:, None] >= boundary[None, :]).astype(jnp.int32), axis=1)
    member = history[:, None] == jnp.arange(lengths_row.shape[0], dtype=jnp.int32)[None, :]
    seq_length = jnp.sum(jnp.where(member, lengths_row[None, :], 0), axis=1).astype(jnp.float32)
    seq_end = jnp.sum(jnp.where(member, boundary[None, :], 0), axis=1)
    seq_start = seq_end - jnp.sum(jnp.where(member, lengths_row[None, :], 0), axis=1)
    return (history, seq_length, seq_start, seq_end)


def on_device(qkvu, actions, lengths, action_table, gain, w_out, cotangent):
    row_total = qkvu.shape[0]
    width = w_out.shape[0]
    heads = width // HD
    scale = HD ** (-0.5)
    lengths_row = lengths[0]
    positions = lax.axis_index("ctx") * row_total + jnp.arange(row_total, dtype=jnp.int32)
    history, seq_length, seq_start, seq_end = history_of(positions, lengths_row)
    raw = qkvu.astype(jnp.float32)
    onehot = (actions[:, None] == jnp.arange(ACTIONS, dtype=jnp.int32)[None, :]).astype(
        jnp.bfloat16
    )
    embedded = jnp.dot(onehot, action_table, preferred_element_type=jnp.float32)
    gate_pre = raw[:, :width] + embedded
    gate = jax.nn.silu(gate_pre)
    value_pre = raw[:, width : 2 * width]
    query_pre = raw[:, 2 * width : 3 * width]
    key_pre = raw[:, 3 * width :]
    values_local = jax.nn.silu(value_pre).astype(jnp.bfloat16)
    queries = jax.nn.silu(query_pre).astype(jnp.bfloat16)
    keys_local = jax.nn.silu(key_pre).astype(jnp.bfloat16)
    query_heads = queries.reshape(row_total, heads, HD)
    key_heads = keys_local.reshape(row_total, heads, HD)
    value_heads = values_local.reshape(row_total, heads, HD)
    whole_keys, whole_values = (
        lax.all_gather(keys_local, "ctx", axis=0, tiled=True),
        lax.all_gather(values_local, "ctx", axis=0, tiled=True),
    )
    amount = whole_keys.shape[0]
    piece_positions = jnp.arange(amount, dtype=jnp.int32)
    piece_history = history_of(piece_positions, lengths_row)[0]
    scores = (
        jnp.einsum(
            "qhd,khd->hqk",
            query_heads,
            whole_keys.reshape(amount, heads, HD),
            preferred_element_type=jnp.float32,
        )
        * scale
    )
    allowed = (history[:, None] == piece_history[None, :]) & (
        piece_positions[None, :] <= positions[:, None]
    )
    weights = jnp.where(allowed[None], jax.nn.silu(scores) / seq_length[None, :, None], 0.0).astype(
        jnp.bfloat16
    )
    summed = jnp.einsum(
        "hqk,khd->qhd",
        weights,
        whole_values.reshape(amount, heads, HD),
        preferred_element_type=jnp.float32,
    )
    attended = summed.reshape(row_total, width)
    centre = attended - jnp.mean(attended, axis=1, keepdims=True)
    inv_std = lax.rsqrt(jnp.mean(centre * centre, axis=1, keepdims=True) + 1e-05)
    normed = centre * inv_std
    mixed = (normed * gain * gate).astype(jnp.bfloat16)
    output = jnp.dot(mixed, w_out, preferred_element_type=jnp.float32).astype(jnp.bfloat16)
    grad_mixed = jnp.einsum("rd,fd->rf", cotangent, w_out, preferred_element_type=jnp.float32)
    weight_term = jnp.einsum("rf,rd->fd", mixed, cotangent, preferred_element_type=jnp.float32)
    gain_term = jnp.sum(grad_mixed * normed * gate, axis=0)
    grad_gate = grad_mixed * gain * normed * silu_slope(gate_pre)
    table_term = jnp.einsum(
        "ra,rf->af", onehot.astype(jnp.float32), grad_gate, precision=lax.Precision.HIGHEST
    )
    pushed = grad_mixed * gain * gate
    grad_out = (
        (
            pushed
            - jnp.mean(pushed, axis=1, keepdims=True)
            - normed * jnp.mean(pushed * normed, axis=1, keepdims=True)
        )
        * inv_std
    ).astype(jnp.bfloat16)
    grad_heads = grad_out.reshape(row_total, heads, HD)
    amount = whole_keys.shape[0]
    piece_positions = jnp.arange(amount, dtype=jnp.int32)
    piece_history = history_of(piece_positions, lengths_row)[0]
    keys_part = whole_keys.reshape(amount, heads, HD)
    scores = (
        jnp.einsum("qhd,khd->hqk", query_heads, keys_part, preferred_element_type=jnp.float32)
        * scale
    )
    allowed = (history[:, None] == piece_history[None, :]) & (
        piece_positions[None, :] <= positions[:, None]
    )
    grad_prod = jnp.einsum(
        "qhd,khd->hqk",
        grad_heads,
        whole_values.reshape(amount, heads, HD),
        preferred_element_type=jnp.float32,
    )
    grad_scores = jnp.where(
        allowed[None], grad_prod * silu_slope(scores) / seq_length[None, :, None], 0.0
    ).astype(jnp.bfloat16)
    summed = jnp.einsum("hqk,khd->qhd", grad_scores, keys_part, preferred_element_type=jnp.float32)
    grad_query = summed.reshape(row_total, width)
    grad_query = grad_query * scale
    piece_queries = lax.all_gather(queries, "ctx", axis=0, tiled=True)
    piece_grads = lax.all_gather(grad_out, "ctx", axis=0, tiled=True)
    amount = piece_queries.shape[0]
    piece_positions = jnp.arange(amount, dtype=jnp.int32)
    piece_info = history_of(piece_positions, lengths_row)
    piece_history = piece_info[0]
    piece_length = piece_info[1]
    queries_part = piece_queries.reshape(amount, heads, HD)
    grads_part = piece_grads.reshape(amount, heads, HD)
    scores = (
        jnp.einsum("qhd,khd->hqk", queries_part, key_heads, preferred_element_type=jnp.float32)
        * scale
    )
    allowed = (piece_history[:, None] == history[None, :]) & (
        positions[None, :] <= piece_positions[:, None]
    )
    weights = jnp.where(
        allowed[None], jax.nn.silu(scores) / piece_length[None, :, None], 0.0
    ).astype(jnp.bfloat16)
    grad_prod = jnp.einsum(
        "qhd,khd->hqk", grads_part, value_heads, preferred_element_type=jnp.float32
    )
    grad_scores = jnp.where(
        allowed[None], grad_prod * silu_slope(scores) / piece_length[None, :, None], 0.0
    ).astype(jnp.bfloat16)
    key_sum = jnp.einsum(
        "hqk,qhd->khd", grad_scores, queries_part, preferred_element_type=jnp.float32
    )
    value_sum = jnp.einsum("hqk,qhd->khd", weights, grads_part, preferred_element_type=jnp.float32)
    grad_key = key_sum.reshape(row_total, width)
    grad_value = value_sum.reshape(row_total, width)
    grad_key = grad_key * scale
    d_qkvu = jnp.concatenate(
        [
            grad_gate,
            grad_value * silu_slope(value_pre),
            grad_query * silu_slope(query_pre),
            grad_key * silu_slope(key_pre),
        ],
        axis=1,
    ).astype(jnp.bfloat16)
    weight_shard = lax.psum_scatter(weight_term, "dp", scatter_dimension=0, tiled=True)
    d_wout, table_group, gain_group = lax.psum((weight_shard, table_term, gain_term), "ctx")
    d_table, d_gain = lax.psum((table_group, gain_group), "dp")
    return (output, d_qkvu, d_wout, d_table, d_gain)


def solution(mesh):
    return jax.shard_map(
        on_device,
        mesh=mesh,
        in_specs=(
            P(("dp", "ctx"), None),
            P(("dp", "ctx")),
            P("dp", None),
            P(),
            P(),
            P(),
            P(("dp", "ctx"), None),
        ),
        out_specs=(P(("dp", "ctx"), None), P(("dp", "ctx"), None), P("dp", None), P(), P()),
        check_vma=False,
    )
```

profile of v0, /device:TPU:0, one launch (start us, length us, event | category | flops | bytes accessed | tf_op | source)
XLA Modules:
  0.0 227.1 jit_solution(12261358709670914872)
XLA Ops:
  7.2 0.9 reduce-window.8
  8.1 0.1 convert_reduce_fusion
  8.2 0.1 convert_reduce_fusion.1
  8.3 0.7 select_reduce_fusion.1
  9.1 0.6 convert_element_type.64
  9.7 0.7 fusion.38
  10.4 1.1 convert_element_type.58
  11.5 0.9 multiply_convert_fusion.6
  12.4 0.6 copy-done.5
  13.0 8.6 %all_gather.12 = bf16[512,512]{1,0:T(8,128)(2,1)S(1)} all-gather(bf16[128,512]{1,0:T(8,128)(2,1)S(1)} %get-tuple-element.17), channel_id=1, replica_groups=mesh['dp'=8,'ctx'=4] {'ctx'}, dimensions={0}, use_global_device_ids=true | all-gather | bytes 655360 | tf_op jit(solution)/shard_map/all_gather | solution.py:51
  21.6 1.0 copy.35
  22.7 7.4 %all_gather.13 = bf16[512,512]{1,0:T(8,128)(2,1)S(1)} all-gather(bf16[128,512]{1,0:T(8,128)(2,1)S(1)} %get-tuple-element.18), channel_id=1, replica_groups=mesh['dp'=8,'ctx'=4] {'ctx'}, dimensions={0}, use_global_device_ids=true | all-gather | bytes 655360 | tf_op jit(solution)/shard_map/all_gather | solution.py:50
  30.1 0.2 copy.36
  30.3 1.2 convolution_multiply_fusion.3
  31.5 2.0 fusion.65
  33.5 0.1 fusion.36
  33.6 0.6 add_rsqrt_fusion
  34.2 0.1 copy.39
  34.4 0.5 fusion.66
  34.9 2.6 %fusion.64 = (bf16[128,512]{1,0:T(8,128)(2,1)}, f32[128,512]{1,0:T(8,128)}, f32[128]{0:T(128)}, f32[128]{0:T(128)}, f32[128,512]{1,0:T(8,128)}, /*index=5*/f32[512]{0:T(512)}, f32[128,512]{1,0:T(8,128)S(1)}) fusion(f32[128]{0:T(128)} %add_rsqrt_fusion, f32[128,512]{1,0:T(8,128)S(1)} %copy.39, f32[128]{0:T(128)S(1)} %broadcast_multiply_fusion.2, ...), kind=kOutput, calls=%fused_computation.102 | convolution fusion | flops 9837824 | bytes 1776128 | tf_op jit(solution)/shard_map/dot_general | solution.py:37
  37.5 0.7 copy-done.8
  38.2 1.9 fusion.63
  40.2 0.1 select_reduce_fusion
  40.3 0.6 convert_element_type.69
  40.9 7.5 %all_gather.15 = bf16[512,512]{1,0:T(8,128)(2,1)S(1)} all-gather(bf16[128,512]{1,0:T(8,128)(2,1)} %get-tuple-element.16), channel_id=1, replica_groups=mesh['dp'=8,'ctx'=4] {'ctx'}, dimensions={0}, use_global_device_ids=true | all-gather | bytes 655360 | tf_op jit(solution)/shard_map/all_gather | solution.py:123
  48.4 1.0 copy.56
  49.4 0.7 broadcast_multiply_fusion
  50.0 1.7 multiply_convert_fusion.3
  51.8 2.9 %fusion.9 = f32[4,128,128]{2,1,0:T(8,128)} fusion(bf16[512,4,128]{0,2,1:T(8,128)(2,1)S(1)} %bitcast.82, bf16[512,4,128]{0,2,1:T(8,128)(2,1)} %bitcast.87, f32[4,128,512]{2,1,0:T(8,128)} %copy-done.3, f32[128]{0:T(128)} %convert_element_type.64, pred[128,512]{1,0:T(8,128)(4,1)} %fusion.38, bf16[128,512]{1,0:T(8,128)(2,1)} %multiply_convert_fusion.3), kind=kOutput, calls=%fused_computation.15 | convolution fusion | flops 137166848 | bytes 2556416 | tf_op jit(solution)/shard_map/hqk,khd->qhd/dot_general | solution.py:120
  54.7 1.1 copy.54
  55.8 7.5 %all_gather.14 = bf16[512,512]{1,0:T(8,128)(2,1)S(1)} all-gather(bf16[128,512]{1,0:T(8,128)(2,1)} %multiply_convert_fusion.3), channel_id=1, replica_groups=mesh['dp'=8,'ctx'=4] {'ctx'}, dimensions={0}, use_global_device_ids=true | all-gather | bytes 655360 | tf_op jit(solution)/shard_map/all_gather | solution.py:124
  63.3 0.8 fusion.39
  64.1 0.3 convolution_multiply_fusion.2
  64.5 1.3 fusion.18
  65.8 1.1 copy.53
  66.9 2.8 %fusion.8 = f32[4,128,128]{2,1,0:T(8,128)} fusion(bf16[512,4,128]{0,2,1:T(8,128)(2,1)S(1)} %bitcast.84, f32[4,512,128]{2,1,0:T(8,128)} %copy-done.4, f32[512]{0:T(512)} %convert_element_type.69, pred[512,128]{1,0:T(8,128)(4,1)} %copy-done.11, bf16[512,512]{1,0:T(8,128)(2,1)} %copy-done.7, bf16[128,512]{1,0:T(8,128)(2,1)S(1)} %copy-done.6), kind=kOutput, calls=%fused_computation.14 | convolution fusion | flops 137166848 | bytes 2557952 | tf_op jit(solution)/shard_map/hqk,qhd->khd/dot_general | solution.py:148
  69.8 1.1 copy.55
  70.8 6.8 %psum.38 = f32[512]{0:T(512)S(1)} all-reduce(f32[512]{0:T(512)S(1)} %copy-done.16), channel_id=1, replica_groups=mesh['dp'=8,'ctx'=4] {'ctx'}, use_global_device_ids=true, to_apply=%region_14.15 | all-reduce | flops 512 | bytes 4096 | tf_op jit(solution)/shard_map/psum | solution.py:165
  77.6 22.4 %psum.39 = f32[512]{0:T(512)} all-reduce(f32[512]{0:T(512)S(1)} %psum.38), channel_id=1, replica_groups=mesh['dp'=8,'ctx'=4] {'dp'}, use_global_device_ids=true, to_apply=%region_15.16 | all-reduce | flops 512 | bytes 4096 | tf_op jit(solution)/shard_map/psum | solution.py:166
  100.0 1.9 fusion.52
  102.0 2.1 convolution_convert_fusion
  104.0 5.2 %reduce-scatter.2.cloned.1.call-done = f32[64,1024]{1,0:T(8,128)} async-done(((f32[512,1024]{1,0:T(8,128)}), f32[64,1024]{1,0:T(8,128)}) %reduce-scatter.2.cloned.1.call-update) | async-done | bytes 262160 | tf_op jit(solution)/shard_map/reduce_scatter | solution.py:164
  109.3 0.3 multiply_convert_fusion.2
  109.6 34.3 %all-reduce.6.cloned.1.call-done = (f32[64,1024]{1,0:T(8,128)}, f32[64,512]{1,0:T(8,128)}) async-done(((f32[64,1024]{1,0:T(8,128)}, f32[64,512]{1,0:T(8,128)}), (f32[64,1024]{1,0:T(8,128)}, f32[64,512]{1,0:T(8,128)})) %all-reduce.6.cloned.1.call-update) | async-done | bytes 393232 | tf_op jit(solution)/shard_map/psum | solution.py:165
  143.9 0.8 pad_maximum_fusion
  144.8 72.5 %all-reduce.4.cloned.1.call-done = f32[64,512]{1,0:T(8,128)} async-done(((f32[64,512]{1,0:T(8,128)}), f32[64,512]{1,0:T(8,128)}) %all-reduce.4.cloned.1.call-update) | async-done | bytes 131088 | tf_op jit(solution)/shard_map/psum | solution.py:166
  217.3 1.7 copy.92
  219.0 1.6 copy.93
  (46 shorter events, 0.3 us)
Async XLA Ops:
  7.2 27.2 %copy-start = (bf16[512,1024]{1,0:T(8,128)(2,1)S(1)}, bf16[512,1024]{1,0:T(8,128)(2,1)}, u32[]{:S(2)}) copy-start(bf16[512,1024]{1,0:T(8,128)(2,1)} %param.12) | copy-start | bytes 3145732
  7.2 102.0 %reduce-scatter.2.cloned.1.call-start = ((), (), s32[]{:S(2)}) async-start(), calls=%async_computation.1 | async-start | bytes 2359296 | tf_op jit(solution)/shard_map/reduce_scatter | solution.py:164
  8.3 14.3 %copy-start.13 = (s32[128]{0:T(128)}, s32[128]{0:T(128)S(1)}, u32[]{:S(2)}) copy-start(s32[128]{0:T(128)S(1)} %convert_reduce_fusion.1) | copy-start | bytes 1540
  12.4 0.6 copy-start.5
  21.6 9.8 %copy-start.19 = (f32[128]{0:T(128)S(1)}, f32[128]{0:T(128)}, u32[]{:S(2)}) copy-start(f32[128]{0:T(128)} %convert_element_type.64) | copy-start | bytes 1540
  22.7 8.8 %copy-start.10 = (pred[128,512]{1,0:T(8,128)(4,1)S(1)}, pred[128,512]{1,0:T(8,128)(4,1)}, u32[]{:S(2)}) copy-start(pred[128,512]{1,0:T(8,128)(4,1)} %fusion.38) | copy-start | bytes 196612
  31.5 2.0 copy-start.3
  31.5 2.9 %copy-start.2 = (bf16[128,1024]{1,0:T(8,128)(2,1)S(1)}, bf16[128,1024]{1,0:T(8,128)(2,1)}, u32[]{:S(2)}) copy-start(bf16[128,1024]{1,0:T(8,128)(2,1)} %param.13) | copy-start | bytes 786436
  33.5 1.4 copy-start.12
  34.4 3.9 %copy-start.14 = (f32[128]{0:T(128)S(1)}, f32[128]{0:T(128)}, u32[]{:S(2)}) copy-start(f32[128]{0:T(128)} %add_rsqrt_fusion) | copy-start | bytes 1540
  37.5 0.7 copy-start.8
  38.2 2.0 copy-start.18
  40.2 103.8 %all-reduce.6.cloned.1.call-start = ((), (), s32[]{:S(2)}) async-start(), calls=%async_computation.3 | async-start | bytes 786432 | tf_op jit(solution)/shard_map/psum | solution.py:165
  51.8 12.3 %copy-start.1 = (bf16[512,512]{0,1:T(8,128)(2,1)S(1)}, bf16[512,512]{0,1:T(8,128)(2,1)}, u32[]{:S(2)}) copy-start(bf16[512,512]{0,1:T(8,128)(2,1)} %copy.56) | copy-start | bytes 1572868
  54.7 9.8 %copy-start.17 = (f32[512]{0:T(512)S(1)}, f32[512]{0:T(512)}, u32[]{:S(2)}) copy-start(f32[512]{0:T(512)} %convert_element_type.69) | copy-start | bytes 6148
  63.3 2.5 %copy-start.7 = (bf16[512,512]{1,0:T(8,128)(2,1)}, bf16[512,512]{1,0:T(8,128)(2,1)S(1)}, u32[]{:S(2)}) copy-start(bf16[512,512]{1,0:T(8,128)(2,1)S(1)} %all_gather.14) | copy-start | bytes 1572868
  64.1 1.7 copy-start.11
  64.5 1.3 copy-start.4
  64.5 2.4 %copy-start.6 = (bf16[128,512]{1,0:T(8,128)(2,1)S(1)}, bf16[128,512]{1,0:T(8,128)(2,1)}, u32[]{:S(2)}) copy-start(bf16[128,512]{1,0:T(8,128)(2,1)} %copy-done.5) | copy-start | bytes 393220
  66.9 4.0 %copy-start.16 = (f32[512]{0:T(512)S(1)}, f32[512]{0:T(512)}, u32[]{:S(2)}) copy-start(f32[512]{0:T(512)} %get-tuple-element.22) | copy-start | bytes 6148
  66.9 35.1 %copy-start.15 = (f32[128]{0:T(128)S(1)}, f32[128]{0:T(128)}, u32[]{:S(2)}) copy-start(f32[128]{0:T(128)} %add_rsqrt_fusion) | copy-start | bytes 1540
  102.0 42.0 %copy-start.9 = (bf16[128,512]{1,0:T(8,128)(2,1)S(1)}, bf16[128,512]{1,0:T(8,128)(2,1)}, u32[]{:S(2)}) copy-start(bf16[128,512]{1,0:T(8,128)(2,1)} %get-tuple-element.10) | copy-start | bytes 393220
  109.3 108.0 %all-reduce.4.cloned.1.call-start = ((), (), s32[]{:S(2)}) async-start(), calls=%async_computation.2 | async-start | bytes 262144 | tf_op jit(solution)/shard_map/psum | solution.py:166
Sparse Core Ops, SparseCore 0:
  40.3 68.8 reduce-scatter.1
  112.3 31.5 all-reduce.5
  147.6 69.6 all-reduce.3
where the time goes:
time: 228 us; the launch traced here: 227 us
  waiting for transfers between devices  112 us (49%)
  blocking collectives  60.2 us (26%)
  matrix products  19.6 us (9%)
  between operations  14 us (6%)
  other arithmetic  10.9 us (5%)
  local copies, waits for them, and re-layouts  10.2 us (4%)
    psum x1, waiting for transfers between devices, on_device(): d_table, d_gain = lax.psum((table_group, gain_group), 'dp')  72.5 us
    psum x1, waiting for transfers between devices, on_device(): lax.psum((weight_shard, table_term, gain_term), 'ctx')  34.3 us
    psum x1, blocking collectives, on_device(): d_table, d_gain = lax.psum((table_group, gain_group), 'dp')  22.4 us
    all_gather x1, blocking collectives, on_device(): lax.all_gather(values_local, 'ctx', axis=0, tiled=True)  8.6 us
    all_gather x1, blocking collectives, on_device(): piece_grads = lax.all_gather(grad_out, 'ctx', axis=0, tiled=True)  7.52 us
    all_gather x1, blocking collectives, on_device(): piece_queries = lax.all_gather(queries, 'ctx', axis=0, tiled=True)  7.48 us
    all_gather x1, blocking collectives, on_device(): lax.all_gather(keys_local, 'ctx', axis=0, tiled=True)  7.41 us
    psum x1, blocking collectives, on_device(): lax.psum((weight_shard, table_term, gain_term), 'ctx')  6.79 us
  transfers between devices with their start and end apart: 3, of which 3 were waited for; matrix products, arithmetic and copies ran while one was open for 9% of the time, Pallas kernels for 0%

commit v1 on v0

v1 whole, which is shorter than its diff:
```python
import functools

import jax
import jax.numpy as jnp
from jax import lax
from jax.experimental import pallas as pl
from jax.experimental.pallas import tpu as pltpu
from jax.sharding import PartitionSpec as P

HD = 128
ACTIONS = 64
F32 = jnp.float32
BF16 = jnp.bfloat16
CTX_KINDS = ("kv", "q", "cot", "mix", "dout", "tab", "gain", "wfin", "tfin")
DP_KINDS = ("wdp", "tdp", "gdp")


def sigmoid(x):
    return 0.5 * jnp.tanh(0.5 * x) + 0.5


def silu_slope(x):
    sig = sigmoid(x)
    return sig * (1.0 + x * (1.0 - sig))


def dot_nn(a, b):
    return lax.dot_general(a, b, (((1,), (0,)), ((), ())), preferred_element_type=F32)


def dot_nt(a, b):
    return lax.dot_general(a, b, (((1,), (1,)), ((), ())), preferred_element_type=F32)


def dot_tn(a, b):
    return lax.dot_general(a, b, (((0,), (0,)), ((), ())), preferred_element_type=F32)


def layer_kernel(
    n_ctx, n_dp, f_parts,
    qkvu_ref, act_ref, len_ref, table_ref, gain_ref, wout_ref, cot_ref,
    out_ref, dqkvu_ref, dwout_ref, dtable_ref, dgain_ref,
    kv_buf, q_buf, cot_buf, mix_buf, do_buf, tab_src, tab_buf, gain_buf,
    wdp_src, wdp_buf, tdp_src, tdp_buf, gdp_src, gdp_buf, wfin_buf, tfin_buf,
    p_q, w_k, p_k, acc, acc_k, acc_v, gm_ref, gate_ref, gslope_ref,
    ctx_send, ctx_recv, dp_send, dp_recv,
):
    me = lax.axis_index("ctx")
    dpi = lax.axis_index("dp")
    rows = qkvu_ref.shape[0]
    width = wout_ref.shape[0]
    heads = width // HD
    scale = HD ** (-0.5)
    c_width = cot_buf.shape[2]
    dp_rows = dwout_ref.shape[0]
    p_rows = dp_rows // f_parts
    t_rows = tab_buf.shape[1]

    def ctx_copy(kind, src, dst, peer):
        k = CTX_KINDS.index(kind)
        return pltpu.make_async_remote_copy(
            src_ref=src, dst_ref=dst,
            send_sem=ctx_send.at[k, peer], recv_sem=ctx_recv.at[k, me],
            device_id={"ctx": peer}, device_id_type=pl.DeviceIdType.MESH,
        )

    def ctx_arrived(kind, buf, source):
        k = CTX_KINDS.index(kind)
        pltpu.make_async_remote_copy(
            src_ref=buf.at[source], dst_ref=buf.at[source],
            send_sem=ctx_send.at[k, source], recv_sem=ctx_recv.at[k, source],
            device_id={"ctx": source}, device_id_type=pl.DeviceIdType.MESH,
        ).wait_recv()

    def dp_copy(kind, src, dst, peer):
        k = DP_KINDS.index(kind)
        return pltpu.make_async_remote_copy(
            src_ref=src, dst_ref=dst,
            send_sem=dp_send.at[k, peer], recv_sem=dp_recv.at[k, dpi],
            device_id={"dp": peer}, device_id_type=pl.DeviceIdType.MESH,
        )

    def dp_arrived(kind, buf, source):
        k = DP_KINDS.index(kind)
        pltpu.make_async_remote_copy(
            src_ref=buf.at[source], dst_ref=buf.at[source],
            send_sem=dp_send.at[k, source], recv_sem=dp_recv.at[k, source],
            device_id={"dp": source}, device_id_type=pl.DeviceIdType.MESH,
        ).wait_recv()

    def ctx_peer(d):
        return lax.rem(me + d, n_ctx)

    def dp_peer(d):
        return lax.rem(dpi + d, n_dp)

    barrier = pltpu.get_barrier_semaphore()
    for d in range(1, n_ctx):
        pl.semaphore_signal(
            barrier, inc=1, device_id={"ctx": ctx_peer(d)}, device_id_type=pl.DeviceIdType.MESH
        )
    for d in range(1, n_dp):
        pl.semaphore_signal(
            barrier, inc=1, device_id={"dp": dp_peer(d)}, device_id_type=pl.DeviceIdType.MESH
        )

    def activated(block):
        x = qkvu_ref[:, block * width : (block + 1) * width].astype(F32)
        return (x * sigmoid(x)).astype(BF16)

    kv_buf[me, :, :width] = activated(3)
    kv_buf[me, :, width:] = activated(1)
    q_buf[me] = activated(2)
    pl.semaphore_wait(barrier, n_ctx - 1 + n_dp - 1)

    def kv_copy(peer):
        return ctx_copy("kv", kv_buf.at[me], kv_buf.at[me], peer)

    def q_copy(peer):
        return ctx_copy("q", q_buf.at[me], q_buf.at[me], peer)

    def do_copy(peer):
        return ctx_copy("dout", do_buf.at[me], do_buf.at[me], peer)

    def cot_copy(peer):
        start = pl.multiple_of((peer // f_parts) * c_width, c_width)
        return ctx_copy("cot", cot_ref.at[:, pl.ds(start, c_width)], cot_buf.at[me], peer)

    def mix_copy(peer):
        return ctx_copy("mix", mix_buf.at[me], mix_buf.at[me], peer)

    def tab_copy(peer):
        return ctx_copy("tab", tab_src.at[peer], tab_buf.at[me], peer)

    def gain_copy(peer):
        return ctx_copy("gain", gain_buf.at[me], gain_buf.at[me], peer)

    def wfin_copy(peer):
        return ctx_copy("wfin", wfin_buf.at[me], wfin_buf.at[me], peer)

    def tfin_copy(peer):
        return ctx_copy("tfin", tfin_buf.at[me], tfin_buf.at[me], peer)

    part = lax.rem(me, f_parts)

    def wdp_copy(peer):
        start = pl.multiple_of(peer * dp_rows + part * p_rows, p_rows)
        return dp_copy("wdp", wdp_src.at[pl.ds(start, p_rows)], wdp_buf.at[dpi], peer)

    def tdp_copy(peer):
        return dp_copy("tdp", tdp_src, tdp_buf.at[dpi], peer)

    def gdp_copy(peer):
        return dp_copy("gdp", gdp_src, gdp_buf.at[dpi], peer)

    def for_higher(action):
        for d in range(1, n_ctx):
            @pl.when(me + d < n_ctx)
            def _():
                action(me + d)

    def for_lower(action):
        for d in range(1, n_ctx):
            @pl.when(me >= d)
            def _():
                action(me - d)

    def for_others(action):
        for d in range(1, n_ctx):
            action(ctx_peer(d))

    def for_dp_others(action):
        for d in range(1, n_dp):
            action(dp_peer(d))

    for_higher(lambda p: kv_copy(p).start())
    for_lower(lambda p: q_copy(p).start())
    for_others(lambda p: cot_copy(p).start())
    own_start = pl.multiple_of((me // f_parts) * c_width, c_width)
    cot_buf[me] = cot_ref[:, pl.ds(own_start, c_width)]

    def history(pos):
        bound = jnp.int32(0)
        start = jnp.zeros_like(pos)
        length = jnp.zeros_like(pos)
        for s in range(len_ref.shape[1]):
            here = pos >= bound
            start = jnp.where(here, bound, start)
            length = jnp.where(here, len_ref[0, s], length)
            bound = bound + len_ref[0, s]
        return start, length

    sub = lax.broadcasted_iota(jnp.int32, (rows, rows), 0)
    lane = lax.broadcasted_iota(jnp.int32, (rows, rows), 1)

    def score_parts(s):
        sig = sigmoid(s)
        t = s * sig
        return t, sig + t * (1.0 - sig)

    def key_side_block(i):
        pos_q = i * rows + lane
        pos_k = me * rows + sub
        start, length = history(pos_q)
        allowed = (pos_k >= start) & (pos_k <= pos_q)
        factor = jnp.where(allowed, 1.0 / length.astype(F32), 0.0)
        for h in range(heads):
            cols = slice(h * HD, (h + 1) * HD)
            t, slope = score_parts(dot_nt(kv_buf[me, :, cols], q_buf[i, :, cols]) * scale)
            w_k[i, h] = (t * factor).astype(BF16)
            p_k[i, h] = slope * factor

    onehot_t = (
        lax.broadcasted_iota(jnp.int32, (ACTIONS, rows), 0) == act_ref[...]
    ).astype(BF16)
    gate_pre = qkvu_ref[:, :width].astype(F32) + dot_tn(onehot_t, table_ref[...])
    gate_sig = sigmoid(gate_pre)
    gate_ref[...] = gate_pre * gate_sig
    gslope_ref[...] = gate_sig * (1.0 + gate_pre * (1.0 - gate_sig))
    gm_ref[...] = dot_nt(cot_ref[...], wout_ref[...])
    key_side_block(me)

    acc[...] = jnp.zeros_like(acc)

    def forward(step, carry):
        j = me - step

        @pl.when(step > 0)
        def _():
            ctx_arrived("kv", kv_buf, j)

        pos_q = me * rows + sub
        pos_k = j * rows + lane
        start, length = history(pos_q)
        allowed = (pos_k >= start) & (pos_k <= pos_q)
        factor = jnp.where(allowed, 1.0 / length.astype(F32), 0.0)
        for h in range(heads):
            cols = slice(h * HD, (h + 1) * HD)
            vcols = slice(width + h * HD, width + (h + 1) * HD)
            t, slope = score_parts(dot_nt(q_buf[me, :, cols], kv_buf[j, :, cols]) * scale)
            p_q[j, h] = slope * factor
            acc[:, cols] += dot_nn((t * factor).astype(BF16), kv_buf[j, :, vcols])
        return carry

    lax.fori_loop(0, me + 1, forward, 0)

    attended = acc[...]
    gain = gain_ref[...]
    gate = gate_ref[...]
    centre = attended - jnp.mean(attended, axis=1, keepdims=True)
    inv_std = lax.rsqrt(jnp.mean(centre * centre, axis=1, keepdims=True) + 1e-05)
    normed = centre * inv_std
    mixed = (normed * gain * gate).astype(BF16)
    mix_buf[me] = mixed
    for_others(lambda p: mix_copy(p).start())
    grad_mixed = gm_ref[...]
    gated = grad_mixed * gate
    pushed = gated * gain
    grad_out = (
        pushed
        - jnp.mean(pushed, axis=1, keepdims=True)
        - normed * jnp.mean(pushed * normed, axis=1, keepdims=True)
    ) * inv_std
    do_buf[me] = grad_out.astype(BF16)
    for_lower(lambda p: do_copy(p).start())
    gain_buf[me] = jnp.sum(gated * normed, axis=0, keepdims=True)
    for_others(lambda p: gain_copy(p).start())
    grad_gate = grad_mixed * gain * normed * gslope_ref[...]
    dqkvu_ref[:, :width] = grad_gate.astype(BF16)
    high = grad_gate.astype(BF16)
    low = (grad_gate - high.astype(F32)).astype(BF16)
    table_term = dot_nn(onehot_t, high) + dot_nn(onehot_t, low)
    for s in range(n_ctx):
        tab_src[s] = table_term[s * t_rows : (s + 1) * t_rows]
    for_others(lambda p: tab_copy(p).start())
    tab_buf[me] = tab_src[me]

    out_ref[...] = dot_nn(mixed, wout_ref[...]).astype(BF16)

    acc[...] = jnp.zeros_like(acc)

    def query_grad(step, carry):
        j = me - step
        for h in range(heads):
            cols = slice(h * HD, (h + 1) * HD)
            vcols = slice(width + h * HD, width + (h + 1) * HD)
            prod = dot_nt(do_buf[me, :, cols], kv_buf[j, :, vcols])
            acc[:, cols] += dot_nn((prod * p_q[j, h]).astype(BF16), kv_buf[j, :, cols])
        return carry

    lax.fori_loop(0, me + 1, query_grad, 0)
    q_pre = qkvu_ref[:, 2 * width : 3 * width].astype(F32)
    dqkvu_ref[:, 2 * width : 3 * width] = (acc[...] * scale * silu_slope(q_pre)).astype(BF16)

    for_others(lambda p: ctx_arrived("gain", gain_buf, p))
    gain_sum = gain_buf[0]
    for s in range(1, n_ctx):
        gain_sum = gain_sum + gain_buf[s]
    gdp_src[...] = gain_sum
    for_dp_others(lambda p: gdp_copy(p).start())
    gdp_buf[dpi] = gain_sum
    for_others(lambda p: ctx_arrived("tab", tab_buf, p))
    tab_sum = tab_buf[0]
    for s in range(1, n_ctx):
        tab_sum = tab_sum + tab_buf[s]
    tdp_src[...] = tab_sum.astype(tdp_src.dtype)
    for_dp_others(lambda p: tdp_copy(p).start())
    tdp_buf[dpi] = tab_sum.astype(tdp_src.dtype)

    def key_side(i, carry):
        ctx_arrived("q", q_buf, i)
        key_side_block(i)
        return carry

    lax.fori_loop(me + 1, n_ctx, key_side, 0)

    for_others(lambda p: ctx_arrived("cot", cot_buf, p))
    for_others(lambda p: ctx_arrived("mix", mix_buf, p))
    w_sum = dot_tn(
        mix_buf[...].reshape(n_ctx * rows, width), cot_buf[...].reshape(n_ctx * rows, c_width)
    )
    wdp_src[...] = w_sum.astype(wdp_src.dtype)
    for_dp_others(lambda p: wdp_copy(p).start())
    own_rows = pl.multiple_of(dpi * dp_rows + part * p_rows, p_rows)
    wdp_buf[dpi] = wdp_src[pl.ds(own_rows, p_rows)]

    acc_k[...] = jnp.zeros_like(acc_k)
    acc_v[...] = jnp.zeros_like(acc_v)

    def key_grad(i, carry):
        @pl.when(i > me)
        def _():
            ctx_arrived("dout", do_buf, i)

        for h in range(heads):
            cols = slice(h * HD, (h + 1) * HD)
            vcols = slice(width + h * HD, width + (h + 1) * HD)
            grads = do_buf[i, :, cols]
            prod = dot_nt(kv_buf[me, :, vcols], grads)
            acc_k[:, cols] += dot_nn((prod * p_k[i, h]).astype(BF16), q_buf[i, :, cols])
            acc_v[:, cols] += dot_nn(w_k[i, h], grads)
        return carry

    lax.fori_loop(me, n_ctx, key_grad, 0)
    v_pre = qkvu_ref[:, width : 2 * width].astype(F32)
    dqkvu_ref[:, width : 2 * width] = (acc_v[...] * silu_slope(v_pre)).astype(BF16)
    k_pre = qkvu_ref[:, 3 * width :].astype(F32)
    dqkvu_ref[:, 3 * width :] = (acc_k[...] * scale * silu_slope(k_pre)).astype(BF16)

    for_dp_others(lambda p: dp_arrived("tdp", tdp_buf, p))
    total = tdp_buf[0].astype(F32)
    for s in range(1, n_dp):
        total = total + tdp_buf[s].astype(F32)
    tfin_buf[me] = total
    for_others(lambda p: tfin_copy(p).start())
    for_dp_others(lambda p: dp_arrived("gdp", gdp_buf, p))
    total = gdp_buf[0]
    for s in range(1, n_dp):
        total = total + gdp_buf[s]
    dgain_ref[...] = total
    for_dp_others(lambda p: dp_arrived("wdp", wdp_buf, p))
    total = wdp_buf[0].astype(F32)
    for s in range(1, n_dp):
        total = total + wdp_buf[s].astype(F32)
    wfin_buf[me] = total.astype(wfin_buf.dtype)
    for_others(lambda p: wfin_copy(p).start())
    for_others(lambda p: ctx_arrived("tfin", tfin_buf, p))
    for s in range(n_ctx):
        dtable_ref[s * t_rows : (s + 1) * t_rows] = tfin_buf[s]
    for_others(lambda p: ctx_arrived("wfin", wfin_buf, p))
    for s in range(n_ctx):
        top, left = (s % f_parts) * p_rows, (s // f_parts) * c_width
        dwout_ref[top : top + p_rows, left : left + c_width] = wfin_buf[s].astype(F32)

    for_higher(lambda p: kv_copy(p).wait_send())
    for_lower(lambda p: q_copy(p).wait_send())
    for_lower(lambda p: do_copy(p).wait_send())
    for copy in (cot_copy, mix_copy, tab_copy, gain_copy, wfin_copy, tfin_copy):
        for_others(lambda p: copy(p).wait_send())
    for copy in (wdp_copy, tdp_copy, gdp_copy):
        for_dp_others(lambda p: copy(p).wait_send())


def on_device(n_ctx, n_dp, qkvu, actions, lengths, action_table, gain, w_out, cotangent):
    rows = qkvu.shape[0]
    width, model = w_out.shape
    heads = width // HD
    c_parts = min(n_ctx, model // 128)
    f_parts = n_ctx // c_parts
    c_width = model // c_parts
    dp_rows = width // n_dp
    p_rows = dp_rows // f_parts
    t_rows = ACTIONS // n_ctx
    w_kind = BF16 if p_rows % 16 == 0 else F32
    t_kind = BF16 if t_rows % 16 == 0 else F32
    vmem = pl.BlockSpec(memory_space=pltpu.VMEM)
    outs = pl.pallas_call(
        functools.partial(layer_kernel, n_ctx, n_dp, f_parts),
        out_shape=(
            jax.ShapeDtypeStruct((rows, model), BF16),
            jax.ShapeDtypeStruct((rows, 4 * width), BF16),
            jax.ShapeDtypeStruct((dp_rows, model), F32),
            jax.ShapeDtypeStruct((ACTIONS, width), F32),
            jax.ShapeDtypeStruct((1, width), F32),
        ),
        in_specs=[vmem, vmem, pl.BlockSpec(memory_space=pltpu.SMEM), vmem, vmem, vmem, vmem],
        out_specs=(vmem,) * 5,
        scratch_shapes=[
            pltpu.VMEM((n_ctx, rows, 2 * width), BF16),
            pltpu.VMEM((n_ctx, rows, width), BF16),
            pltpu.VMEM((n_ctx, rows, c_width), BF16),
            pltpu.VMEM((n_ctx, rows, width), BF16),
            pltpu.VMEM((n_ctx, rows, width), BF16),
            pltpu.VMEM((n_ctx, t_rows, width), F32),
            pltpu.VMEM((n_ctx, t_rows, width), F32),
            pltpu.VMEM((n_ctx, 1, width), F32),
            pltpu.VMEM((width, c_width), w_kind),
            pltpu.VMEM((n_dp, p_rows, c_width), w_kind),
            pltpu.VMEM((t_rows, width), t_kind),
            pltpu.VMEM((n_dp, t_rows, width), t_kind),
            pltpu.VMEM((1, width), F32),
            pltpu.VMEM((n_dp, 1, width), F32),
            pltpu.VMEM((n_ctx, p_rows, c_width), w_kind),
            pltpu.VMEM((n_ctx, t_rows, width), F32),
            pltpu.VMEM((n_ctx, heads, rows, rows), F32),
            pltpu.VMEM((n_ctx, heads, rows, rows), BF16),
            pltpu.VMEM((n_ctx, heads, rows, rows), F32),
            pltpu.VMEM((rows, width), F32),
            pltpu.VMEM((rows, width), F32),
            pltpu.VMEM((rows, width), F32),
            pltpu.VMEM((rows, width), F32),
            pltpu.VMEM((rows, width), F32),
            pltpu.VMEM((rows, width), F32),
            pltpu.SemaphoreType.DMA((len(CTX_KINDS), n_ctx)),
            pltpu.SemaphoreType.DMA((len(CTX_KINDS), n_ctx)),
            pltpu.SemaphoreType.DMA((len(DP_KINDS), n_dp)),
            pltpu.SemaphoreType.DMA((len(DP_KINDS), n_dp)),
        ],
        compiler_params=pltpu.CompilerParams(
            collective_id=0, has_side_effects=True, vmem_limit_bytes=48 * 1024 * 1024
        ),
        name="attention_layer",
    )(
        qkvu, actions.reshape(1, rows), lengths, action_table,
        gain.reshape(1, width), w_out, cotangent,
    )
    output, d_qkvu, d_wout, d_table, d_gain = outs
    return output, d_qkvu, d_wout, d_table, d_gain.reshape(width)


def solution(mesh):
    both = P(("dp", "ctx"), None)
    return jax.shard_map(
        functools.partial(on_device, mesh.shape["ctx"], mesh.shape["dp"]),
        mesh=mesh,
        in_specs=(both, P(("dp", "ctx")), P("dp", None), P(), P(), P(), both),
        out_specs=(both, both, P("dp", None), P(), P()),
        check_vma=False,
    )
```

time: 228 us -> 51.5 us (0.23)
  waiting for transfers between devices: 112 us -> 0 us
  blocking collectives: 60.2 us -> 0 us
  Pallas kernels: 0 us -> 42.3 us
  matrix products: 19.6 us -> 0 us
  between operations: 14 us -> 0.67 us
  other arithmetic: 10.9 us -> 0 us
    psum x2 -> x0, waiting for transfers between devices: 107 us -> none  [the longest x1 72.5 us: on_device(): d_table, d_gain = lax.psum((table_group, gain_group), 'dp')]
    pallas_call x0 -> x1, Pallas kernels: none -> 42.3 us  [on_device(): pl.pallas_call(functools.partial(layer_kernel, n_ctx, n_dp, f_parts), out...]
    all_gather x4 -> x0, blocking collectives: 31 us -> none  [the longest x1 8.6 us: on_device(): lax.all_gather(values_local, 'ctx', axis=0, tiled=True)]
    psum x2 -> x0, blocking collectives: 29.2 us -> none  [the longest x1 22.4 us: on_device(): d_table, d_gain = lax.psum((table_group, gain_group), 'dp')]
    dot_general x11 -> x0, matrix products: 19.6 us -> none  [the longest x1 2.92 us: on_device(): jnp.einsum('hqk,khd->qhd', grad_scores, keys_part, preferred_element_type...]
    reduce_scatter x1 -> x0, waiting for transfers between devices: 5.18 us -> none  [on_device(): lax.psum_scatter(weight_term, 'dp', scatter_dimension=0, tiled=True)]
    convert_element_type x5 -> x0, other arithmetic: 4.93 us -> none  [the longest x1 1.75 us: on_device(): grad_out = ((pushed - jnp.mean(pushed, axis=1, keepdims=True) - normed *...]
    unnamed x42 -> x19, local copies, waits for them, and re-layouts: 4.67 us -> 8.15 us
  transfers between devices with their start and end apart: 3 -> 0, of which waited for: 3 -> 0; matrix products, arithmetic and copies ran while one was open for 9% -> 0% of each run, Pallas kernels for 0% -> 0%
where the time goes in v1:
time: 51.5 us; the launch traced here: 51.1 us
  Pallas kernels  42.3 us (82%)
  local copies, waits for them, and re-layouts  8.15 us (16%)
  between operations  0.67 us (1%)
    pallas_call x1, Pallas kernels, on_device(): pl.pallas_call(functools.partial(layer_kernel, n_ctx, n_dp, f_parts), out...  42.3 us
    unnamed x19, local copies, waits for them, and re-layouts  8.15 us

profile of v1, /device:TPU:0, one launch (start us, length us, event | category | flops | bytes accessed | tf_op | source)
XLA Modules:
  0.0 51.1 jit_solution(6794825384255826544)
XLA Ops:
  0.6 0.0 copy-start.4
  0.6 0.0 copy-start.5
  0.7 0.0 copy-start.6
  0.7 0.7 %copy-done.4 = f32[512]{0:T(512)S(1)} copy-done((f32[512]{0:T(512)S(1)}, f32[512]{0:T(512)}, u32[]{:S(2)}) %copy-start.4) | copy-done | bytes 2072
  1.3 0.0 copy-done.5
  1.3 0.0 copy-done.6
  1.3 0.0 copy-start
  1.3 1.2 %copy-done = bf16[512,1024]{1,0:T(8,128)(2,1)S(1)} copy-done((bf16[512,1024]{1,0:T(8,128)(2,1)S(1)}, bf16[512,1024]{1,0:T(8,128)(2,1)}, u32[]{:S(2)}) %copy-start) | copy-done | bytes 1048600
  2.5 0.0 copy-start.1
  2.5 1.0 %copy-done.1 = bf16[128,2048]{1,0:T(8,128)(2,1)S(1)} copy-done((bf16[128,2048]{1,0:T(8,128)(2,1)S(1)}, bf16[128,2048]{1,0:T(8,128)(2,1)}, u32[]{:S(2)}) %copy-start.1) | copy-done | bytes 524312
  3.6 0.0 copy-start.2
  3.6 0.9 %copy-done.2 = bf16[128,1024]{1,0:T(8,128)(2,1)S(1)} copy-done((bf16[128,1024]{1,0:T(8,128)(2,1)S(1)}, bf16[128,1024]{1,0:T(8,128)(2,1)}, u32[]{:S(2)}) %copy-start.2) | copy-done | bytes 262168
  4.5 0.0 copy-start.3
  4.5 0.8 %copy-done.3 = bf16[64,512]{1,0:T(8,128)(2,1)S(1)} copy-done((bf16[64,512]{1,0:T(8,128)(2,1)S(1)}, bf16[64,512]{1,0:T(8,128)(2,1)}, u32[]{:S(2)}) %copy-start.3) | copy-done | bytes 65560
  5.4 42.3 %attention_layer.1 = (bf16[128,1024]{1,0:T(8,128)(2,1)S(1)}, bf16[128,2048]{1,0:T(8,128)(2,1)S(1)}, f32[64,1024]{1,0:T(8,128)S(1)}, f32[64,512]{1,0:T(8,128)S(1)}, f32[1,512]{1,0:T(1,128)S(1)}) custom-call(bf16[128,2048]{1,0:T(8,128)(2,1)S(1)} %copy-done.1, s32[1,128]{1,0:T(1,128)S(1)} %bitcast.5, s32[1,4]{1,0:T(1,128)S(1)} %copy-done.6, ...), custom_call_target="tpu_custom_call" | custom-call | tf_op jit(solution)/shard_map/attention_layer/pallas_call | solution.py:397
  47.7 0.7 %copy.17 = bf16[128,1024]{1,0:T(8,128)(2,1)} copy(bf16[128,1024]{1,0:T(8,128)(2,1)S(1)} %get-tuple-element.20) | data formatting | bytes 524288
  48.4 0.8 %copy.18 = bf16[128,2048]{1,0:T(8,128)(2,1)} copy(bf16[128,2048]{1,0:T(8,128)(2,1)S(1)} %get-tuple-element.21) | data formatting | bytes 1048576
  49.2 0.7 %copy.19 = f32[64,1024]{1,0:T(8,128)} copy(f32[64,1024]{1,0:T(8,128)S(1)} %get-tuple-element.22) | data formatting | bytes 524288
  49.9 0.7 %copy.20 = f32[64,512]{1,0:T(8,128)} copy(f32[64,512]{1,0:T(8,128)S(1)} %get-tuple-element.23) | data formatting | bytes 262144
  50.5 0.6 %copy.21 = f32[512]{0:T(512)} copy(f32[512]{0:T(512)S(1)} %bitcast.3) | data formatting | bytes 4096
Async XLA Ops:
  0.6 0.7 %copy-start.4 = (f32[512]{0:T(512)S(1)}, f32[512]{0:T(512)}, u32[]{:S(2)}) copy-start(f32[512]{0:T(512)} %param.11) | copy-start | bytes 6148
  0.6 0.7 %copy-start.5 = (s32[128]{0:T(128)S(1)}, s32[128]{0:T(128)}, u32[]{:S(2)}) copy-start(s32[128]{0:T(128)} %param.8) | copy-start | bytes 1540
  0.7 0.7 %copy-start.6 = (s32[1,4]{1,0:T(1,128)S(1)}, s32[1,4]{1,0:T(1,128)}, u32[]{:S(2)}) copy-start(s32[1,4]{1,0:T(1,128)} %len_ref.1) | copy-start | bytes 52
  1.3 1.2 %copy-start = (bf16[512,1024]{1,0:T(8,128)(2,1)S(1)}, bf16[512,1024]{1,0:T(8,128)(2,1)}, u32[]{:S(2)}) copy-start(bf16[512,1024]{1,0:T(8,128)(2,1)} %wout_ref.1) | copy-start | bytes 3145732
  2.5 1.0 %copy-start.1 = (bf16[128,2048]{1,0:T(8,128)(2,1)S(1)}, bf16[128,2048]{1,0:T(8,128)(2,1)}, u32[]{:S(2)}) copy-start(bf16[128,2048]{1,0:T(8,128)(2,1)} %qkvu_ref.1) | copy-start | bytes 1572868
  3.6 0.9 %copy-start.2 = (bf16[128,1024]{1,0:T(8,128)(2,1)S(1)}, bf16[128,1024]{1,0:T(8,128)(2,1)}, u32[]{:S(2)}) copy-start(bf16[128,1024]{1,0:T(8,128)(2,1)} %cot_ref.1) | copy-start | bytes 786436
  4.5 0.8 %copy-start.3 = (bf16[64,512]{1,0:T(8,128)(2,1)S(1)}, bf16[64,512]{1,0:T(8,128)(2,1)}, u32[]{:S(2)}) copy-start(bf16[64,512]{1,0:T(8,128)(2,1)} %table_ref.1) | copy-start | bytes 196612

commit v2 on v1

--- a/solution.py
+++ b/solution.py
@@ -38,12 +38,13 @@
 
 def layer_kernel(
     n_ctx, n_dp, f_parts,
-    qkvu_ref, act_ref, len_ref, table_ref, gain_ref, wout_ref, cot_ref,
+    qkvu_in, act_in, len_in, table_in, gain_in, wout_in, cot_in,
     out_ref, dqkvu_ref, dwout_ref, dtable_ref, dgain_ref,
     kv_buf, q_buf, cot_buf, mix_buf, do_buf, tab_src, tab_buf, gain_buf,
     wdp_src, wdp_buf, tdp_src, tdp_buf, gdp_src, gdp_buf, wfin_buf, tfin_buf,
     p_q, w_k, p_k, acc, acc_k, acc_v, gm_ref, gate_ref, gslope_ref,
-    ctx_send, ctx_recv, dp_send, dp_recv,
+    qkvu_ref, act_ref, len_ref, table_ref, gain_ref, wout_ref, cot_ref,
+    ctx_send, ctx_recv, relay_send, dp_send, dp_recv, load_sem,
 ):
     me = lax.axis_index("ctx")
     dpi = lax.axis_index("dp")
@@ -94,6 +95,34 @@
     def dp_peer(d):
         return lax.rem(dpi + d, n_dp)
 
+    core = lax.rem(me, 2)
+    chip = me // 2
+    chips = n_ctx // 2
+    sibling = me + 1 - 2 * core
+
+    def relay_copy(kind, buf, slot):
+        k = CTX_KINDS.index(kind)
+        return pltpu.make_async_remote_copy(
+            src_ref=buf.at[slot], dst_ref=buf.at[slot],
+            send_sem=relay_send.at[k, slot], recv_sem=ctx_recv.at[k, slot],
+            device_id={"ctx": sibling}, device_id_type=pl.DeviceIdType.MESH,
+        )
+
+    def relay(kind, buf, low, high):
+        def step(c, carry):
+            ctx_arrived(kind, buf, 2 * c + core)
+            relay_copy(kind, buf, 2 * c + core).start()
+            return carry
+
+        lax.fori_loop(low, high, step, 0)
+
+    def relay_wait(kind, buf, low, high):
+        def step(c, carry):
+            relay_copy(kind, buf, 2 * c + core).wait_send()
+            return carry
+
+        lax.fori_loop(low, high, step, 0)
+
     barrier = pltpu.get_barrier_semaphore()
     for d in range(1, n_ctx):
         pl.semaphore_signal(
@@ -104,13 +133,30 @@
             barrier, inc=1, device_id={"dp": dp_peer(d)}, device_id_type=pl.DeviceIdType.MESH
         )
 
+    qkvu_cols = [slice(b * width, (b + 1) * width) for b in range(4)]
+    loads = [
+        pltpu.make_async_copy(source, target, load_sem.at[n])
+        for n, (source, target) in enumerate(
+            [(qkvu_in.at[:, qkvu_cols[b]], qkvu_ref.at[:, qkvu_cols[b]]) for b in (3, 1, 2)]
+            + [(cot_in, cot_ref), (wout_in, wout_ref), (len_in, len_ref)]
+            + [(qkvu_in.at[:, qkvu_cols[0]], qkvu_ref.at[:, qkvu_cols[0]])]
+            + [(table_in, table_ref), (act_in, act_ref), (gain_in, gain_ref)]
+        )
+    ]
+    for load in loads:
+        load.start()
+
     def activated(block):
         x = qkvu_ref[:, block * width : (block + 1) * width].astype(F32)
         return (x * sigmoid(x)).astype(BF16)
 
+    loads[0].wait()
     kv_buf[me, :, :width] = activated(3)
+    loads[1].wait()
     kv_buf[me, :, width:] = activated(1)
+    loads[2].wait()
     q_buf[me] = activated(2)
+    loads[3].wait()
     pl.semaphore_wait(barrier, n_ctx - 1 + n_dp - 1)
 
     def kv_copy(peer):
@@ -154,16 +200,29 @@
         return dp_copy("gdp", gdp_src, gdp_buf.at[dpi], peer)
 
     def for_higher(action):
-        for d in range(1, n_ctx):
-            @pl.when(me + d < n_ctx)
+        @pl.when(core == 0)
+        def _():
+            action(sibling)
+
+        for d in range(1, chips):
+            @pl.when(chip + d < chips)
             def _():
-                action(me + d)
+                action(me + 2 * d)
 
     def for_lower(action):
-        for d in range(1, n_ctx):
-            @pl.when(me >= d)
+        @pl.when(core == 1)
+        def _():
+            action(sibling)
+
+        for d in range(1, chips):
+            @pl.when(chip >= d)
             def _():
-                action(me - d)
+                action(me - 2 * d)
+
+    def for_partners(action):
+        for d in range(1, chips):
+            action(ctx_peer(2 * d))
+        action(sibling)
 
     def for_others(action):
         for d in range(1, n_ctx):
@@ -210,6 +269,9 @@
             w_k[i, h] = (t * factor).astype(BF16)
             p_k[i, h] = slope * factor
 
+    for load in loads[4:]:
+        load.wait()
+
     onehot_t = (
         lax.broadcasted_iota(jnp.int32, (ACTIONS, rows), 0) == act_ref[...]
     ).astype(BF16)
@@ -222,13 +284,7 @@
 
     acc[...] = jnp.zeros_like(acc)
 
-    def forward(step, carry):
-        j = me - step
-
-        @pl.when(step > 0)
-        def _():
-            ctx_arrived("kv", kv_buf, j)
-
+    def forward(j):
         pos_q = me * rows + sub
         pos_k = j * rows + lane
         start, length = history(pos_q)
@@ -240,9 +296,26 @@
             t, slope = score_parts(dot_nt(q_buf[me, :, cols], kv_buf[j, :, cols]) * scale)
             p_q[j, h] = slope * factor
             acc[:, cols] += dot_nn((t * factor).astype(BF16), kv_buf[j, :, vcols])
-        return carry
-
-    lax.fori_loop(0, me + 1, forward, 0)
+
+    def forward_direct(c, carry):
+        forward(2 * c + core)
+        return carry
+
+    def forward_relayed(c, carry):
+        ctx_arrived("kv", kv_buf, 2 * c + 1 - core)
+        forward(2 * c + 1 - core)
+        return carry
+
+    lax.fori_loop(chip, chip + 1, forward_direct, 0)
+
+    @pl.when(core == 1)
+    def _():
+        ctx_arrived("kv", kv_buf, sibling)
+        forward(sibling)
+
+    relay("kv", kv_buf, 0, chip)
+    lax.fori_loop(0, chip, forward_direct, 0)
+    lax.fori_loop(0, chip, forward_relayed, 0)
 
     attended = acc[...]
     gain = gain_ref[...]
@@ -252,7 +325,7 @@
     normed = centre * inv_std
     mixed = (normed * gain * gate).astype(BF16)
     mix_buf[me] = mixed
-    for_others(lambda p: mix_copy(p).start())
+    for_partners(lambda p: mix_copy(p).start())
     grad_mixed = gm_ref[...]
     gated = grad_mixed * gate
     pushed = gated * gain
@@ -263,6 +336,7 @@
     ) * inv_std
     do_buf[me] = grad_out.astype(BF16)
     for_lower(lambda p: do_copy(p).start())
+    relay("mix", mix_buf, 0, chip)
     gain_buf[me] = jnp.sum(gated * normed, axis=0, keepdims=True)
     for_others(lambda p: gain_copy(p).start())
     grad_gate = grad_mixed * gain * normed * gslope_ref[...]
@@ -274,6 +348,7 @@
         tab_src[s] = table_term[s * t_rows : (s + 1) * t_rows]
     for_others(lambda p: tab_copy(p).start())
     tab_buf[me] = tab_src[me]
+    relay("q", q_buf, chip + 1, chips)
 
     out_ref[...] = dot_nn(mixed, wout_ref[...]).astype(BF16)
 
@@ -291,6 +366,24 @@
     lax.fori_loop(0, me + 1, query_grad, 0)
     q_pre = qkvu_ref[:, 2 * width : 3 * width].astype(F32)
     dqkvu_ref[:, 2 * width : 3 * width] = (acc[...] * scale * silu_slope(q_pre)).astype(BF16)
+
+    @pl.when(core == 0)
+    def _():
+        ctx_arrived("q", q_buf, sibling)
+        key_side_block(sibling)
+
+    def key_side_direct(c, carry):
+        key_side_block(2 * c + core)
+        return carry
+
+    def key_side_relayed(c, carry):
+        ctx_arrived("q", q_buf, 2 * c + 1 - core)
+        key_side_block(2 * c + 1 - core)
+        return carry
+
+    lax.fori_loop(chip + 1, chips, key_side_direct, 0)
+    lax.fori_loop(chip + 1, chips, key_side_relayed, 0)
+    relay("mix", mix_buf, chip + 1, chips)
 
     for_others(lambda p: ctx_arrived("gain", gain_buf, p))
     gain_sum = gain_buf[0]
@@ -307,15 +400,10 @@
     for_dp_others(lambda p: tdp_copy(p).start())
     tdp_buf[dpi] = tab_sum.astype(tdp_src.dtype)
 
-    def key_side(i, carry):
-        ctx_arrived("q", q_buf, i)
-        key_side_block(i)
-        return carry
-
-    lax.fori_loop(me + 1, n_ctx, key_side, 0)
-
     for_others(lambda p: ctx_arrived("cot", cot_buf, p))
-    for_others(lambda p: ctx_arrived("mix", mix_buf, p))
+    ctx_arrived("mix", mix_buf, sibling)
+    for d in range(1, chips):
+        ctx_arrived("mix", mix_buf, lax.rem(sibling + 2 * d, n_ctx))
     w_sum = dot_tn(
         mix_buf[...].reshape(n_ctx * rows, width), cot_buf[...].reshape(n_ctx * rows, c_width)
     )
@@ -327,11 +415,7 @@
     acc_k[...] = jnp.zeros_like(acc_k)
     acc_v[...] = jnp.zeros_like(acc_v)
 
-    def key_grad(i, carry):
-        @pl.when(i > me)
-        def _():
-            ctx_arrived("dout", do_buf, i)
-
+    def key_grad(i):
         for h in range(heads):
             cols = slice(h * HD, (h + 1) * HD)
             vcols = slice(width + h * HD, width + (h + 1) * HD)
@@ -339,9 +423,19 @@
             prod = dot_nt(kv_buf[me, :, vcols], grads)
             acc_k[:, cols] += dot_nn((prod * p_k[i, h]).astype(BF16), q_buf[i, :, cols])
             acc_v[:, cols] += dot_nn(w_k[i, h], grads)
-        return carry
-
-    lax.fori_loop(me, n_ctx, key_grad, 0)
+
+    def key_grad_direct(c, carry):
+        key_grad(2 * c + core)
+        return carry
+
+    def key_grad_relayed(c, carry):
+        ctx_arrived("dout", do_buf, 2 * c + 1 - core)
+        key_grad(2 * c + 1 - core)
+        return carry
+
+    relay("dout", do_buf, chip + 1, chips)
+    lax.fori_loop(chip, chips, key_grad_direct, 0)
+    lax.fori_loop(chip + core, chips, key_grad_relayed, 0)
     v_pre = qkvu_ref[:, width : 2 * width].astype(F32)
     dqkvu_ref[:, width : 2 * width] = (acc_v[...] * silu_slope(v_pre)).astype(BF16)
     k_pre = qkvu_ref[:, 3 * width :].astype(F32)
@@ -375,10 +469,25 @@
     for_higher(lambda p: kv_copy(p).wait_send())
     for_lower(lambda p: q_copy(p).wait_send())
     for_lower(lambda p: do_copy(p).wait_send())
-    for copy in (cot_copy, mix_copy, tab_copy, gain_copy, wfin_copy, tfin_copy):
+    for_partners(lambda p: mix_copy(p).wait_send())
+    relay_wait("kv", kv_buf, 0, chip)
+    relay_wait("q", q_buf, chip + 1, chips)
+    relay_wait("dout", do_buf, chip + 1, chips)
+    relay_wait("mix", mix_buf, 0, chip)
+    relay_wait("mix", mix_buf, chip + 1, chips)
+    for copy in (cot_copy, tab_copy, gain_copy, wfin_copy, tfin_copy):
         for_others(lambda p: copy(p).wait_send())
     for copy in (wdp_copy, tdp_copy, gdp_copy):
         for_dp_others(lambda p: copy(p).wait_send())
+
+
+def store_kernel(*refs):
+    sems = refs[10]
+    stores = [pltpu.make_async_copy(refs[n], refs[5 + n], sems.at[n]) for n in range(5)]
+    for store in stores:
+        store.start()
+    for store in stores:
+        store.wait()
 
 
 def on_device(n_ctx, n_dp, qkvu, actions, lengths, action_table, gain, w_out, cotangent):
@@ -403,7 +512,7 @@
             jax.ShapeDtypeStruct((ACTIONS, width), F32),
             jax.ShapeDtypeStruct((1, width), F32),
         ),
-        in_specs=[vmem, vmem, pl.BlockSpec(memory_space=pltpu.SMEM), vmem, vmem, vmem, vmem],
+        in_specs=[pl.BlockSpec(memory_space=pltpu.HBM)] * 7,
         out_specs=(vmem,) * 5,
         scratch_shapes=[
             pltpu.VMEM((n_ctx, rows, 2 * width), BF16),
@@ -431,10 +540,19 @@
             pltpu.VMEM((rows, width), F32),
             pltpu.VMEM((rows, width), F32),
             pltpu.VMEM((rows, width), F32),
+            pltpu.VMEM((rows, 4 * width), BF16),
+            pltpu.VMEM((1, rows), jnp.int32),
+            pltpu.SMEM(lengths.shape, jnp.int32),
+            pltpu.VMEM(action_table.shape, BF16),
+            pltpu.VMEM((1, width), F32),
+            pltpu.VMEM((width, model), BF16),
+            pltpu.VMEM((rows, model), BF16),
+            pltpu.SemaphoreType.DMA((len(CTX_KINDS), n_ctx)),
             pltpu.SemaphoreType.DMA((len(CTX_KINDS), n_ctx)),
             pltpu.SemaphoreType.DMA((len(CTX_KINDS), n_ctx)),
             pltpu.SemaphoreType.DMA((len(DP_KINDS), n_dp)),
             pltpu.SemaphoreType.DMA((len(DP_KINDS), n_dp)),
+            pltpu.SemaphoreType.DMA((10,)),
         ],
         compiler_params=pltpu.CompilerParams(
             collective_id=0, has_side_effects=True, vmem_limit_bytes=48 * 1024 * 1024
@@ -444,7 +562,14 @@
         qkvu, actions.reshape(1, rows), lengths, action_table,
         gain.reshape(1, width), w_out, cotangent,
     )
-    output, d_qkvu, d_wout, d_table, d_gain = outs
+    output, d_qkvu, d_wout, d_table, d_gain = pl.pallas_call(
+        store_kernel,
+        out_shape=[jax.ShapeDtypeStruct(o.shape, o.dtype) for o in outs],
+        in_specs=[vmem] * 5,
+        out_specs=[pl.BlockSpec(memory_space=pl.ANY)] * 5,
+        scratch_shapes=[pltpu.SemaphoreType.DMA((5,))],
+        name="store_results",
+    )(*outs)
     return output, d_qkvu, d_wout, d_table, d_gain.reshape(width)
 
 

time: 51.5 us -> 48.7 us (0.946)
  Pallas kernels: 42.3 us -> 39.2 us
    pallas_call x1, Pallas kernels: 42.3 us -> 36.9 us  [on_device(): pl.pallas_call(functools.partial(layer_kernel, n_ctx, n_dp, f_parts), out...]
    pallas_call x0 -> x1, Pallas kernels: none -> 2.27 us  [on_device(): pl.pallas_call(store_kernel, out_shape=[jax.ShapeDtypeStruct(o.shape, o.d...]
    unnamed x19 -> x24, local copies, waits for them, and re-layouts: 8.15 us -> 8.16 us
where the time goes in v2:
time: 48.7 us; the launch traced here: 48 us
  Pallas kernels  39.2 us (80%)
  local copies, waits for them, and re-layouts  8.16 us (17%)
  between operations  0.68 us (1%)
    pallas_call x1, Pallas kernels, on_device(): pl.pallas_call(functools.partial(layer_kernel, n_ctx, n_dp, f_parts), out...  36.9 us
    unnamed x24, local copies, waits for them, and re-layouts  8.16 us
    pallas_call x1, Pallas kernels, on_device(): pl.pallas_call(store_kernel, out_shape=[jax.ShapeDtypeStruct(o.shape, o.d...  2.27 us

profile of v2, /device:TPU:0, one launch (start us, length us, event | category | flops | bytes accessed | tf_op | source)
XLA Modules:
  0.0 48.0 jit_solution(6008896735873667645)
XLA Ops:
  0.6 0.0 copy-start.9
  0.6 0.0 copy-start.10
  0.7 0.0 copy-start.11
  0.7 0.7 %copy-done.9 = f32[512]{0:T(512)S(1)} copy-done((f32[512]{0:T(512)S(1)}, f32[512]{0:T(512)}, u32[]{:S(2)}) %copy-start.9) | copy-done | bytes 2072
  1.3 0.0 copy-done.10
  1.3 0.0 copy-done.11
  1.3 0.0 copy-start
  1.3 1.2 %copy-done = bf16[512,1024]{1,0:T(8,128)(2,1)S(1)} copy-done((bf16[512,1024]{1,0:T(8,128)(2,1)S(1)}, bf16[512,1024]{1,0:T(8,128)(2,1)}, u32[]{:S(2)}) %copy-start) | copy-done | bytes 1048600
  2.5 0.0 copy-start.2
  2.5 1.0 %copy-done.2 = bf16[128,2048]{1,0:T(8,128)(2,1)S(1)} copy-done((bf16[128,2048]{1,0:T(8,128)(2,1)S(1)}, bf16[128,2048]{1,0:T(8,128)(2,1)}, u32[]{:S(2)}) %copy-start.2) | copy-done | bytes 524312
  3.6 0.0 copy-start.3
  3.6 0.9 %copy-done.3 = bf16[128,1024]{1,0:T(8,128)(2,1)S(1)} copy-done((bf16[128,1024]{1,0:T(8,128)(2,1)S(1)}, bf16[128,1024]{1,0:T(8,128)(2,1)}, u32[]{:S(2)}) %copy-start.3) | copy-done | bytes 262168
  4.5 0.0 copy-start.7
  4.5 0.8 %copy-done.7 = bf16[64,512]{1,0:T(8,128)(2,1)S(1)} copy-done((bf16[64,512]{1,0:T(8,128)(2,1)S(1)}, bf16[64,512]{1,0:T(8,128)(2,1)}, u32[]{:S(2)}) %copy-start.7) | copy-done | bytes 65560
  5.4 36.9 %attention_layer.1 = (bf16[128,1024]{1,0:T(8,128)(2,1)S(1)}, bf16[128,2048]{1,0:T(8,128)(2,1)S(1)}, f32[64,1024]{1,0:T(8,128)S(1)}, f32[64,512]{1,0:T(8,128)S(1)}, f32[1,512]{1,0:T(1,128)S(1)}) custom-call(bf16[128,2048]{1,0:T(8,128)(2,1)S(1)} %copy-done.2, s32[1,128]{1,0:T(1,128)S(1)} %bitcast.4, s32[1,4]{1,0:T(1,128)S(1)} %copy-done.11, ...), custom_call_target="tpu_custom_call" | custom-call | tf_op jit(solution)/shard_map/attention_layer/pallas_call | solution.py:506
  42.3 0.0 copy-start.1
  42.3 0.8 %copy-done.1 = bf16[128,2048]{1,0:T(8,128)(2,1)} copy-done((bf16[128,2048]{1,0:T(8,128)(2,1)}, bf16[128,2048]{1,0:T(8,128)(2,1)S(1)}, u32[]{:S(2)}) %copy-start.1) | copy-done | bytes 524312
  43.1 0.0 copy-start.4
  43.1 0.7 %copy-done.4 = bf16[128,1024]{1,0:T(8,128)(2,1)} copy-done((bf16[128,1024]{1,0:T(8,128)(2,1)}, bf16[128,1024]{1,0:T(8,128)(2,1)S(1)}, u32[]{:S(2)}) %copy-start.4) | copy-done | bytes 262168
  43.8 0.0 copy-start.5
  43.8 0.7 %copy-done.5 = f32[64,1024]{1,0:T(8,128)} copy-done((f32[64,1024]{1,0:T(8,128)}, f32[64,1024]{1,0:T(8,128)S(1)}, u32[]{:S(2)}) %copy-start.5) | copy-done | bytes 262168
  44.5 0.0 copy-start.6
  44.5 0.6 %copy-done.6 = f32[64,512]{1,0:T(8,128)} copy-done((f32[64,512]{1,0:T(8,128)}, f32[64,512]{1,0:T(8,128)S(1)}, u32[]{:S(2)}) %copy-start.6) | copy-done | bytes 131096
  45.2 0.0 copy-start.8
  45.2 0.6 %copy-done.8 = f32[1,512]{1,0:T(1,128)} copy-done((f32[1,512]{1,0:T(1,128)}, f32[1,512]{1,0:T(1,128)S(1)}, u32[]{:S(2)}) %copy-start.8) | copy-done | bytes 2072
  45.8 2.3 %store_results.1 = (bf16[128,1024]{1,0:T(8,128)(2,1)}, bf16[128,2048]{1,0:T(8,128)(2,1)}, f32[64,1024]{1,0:T(8,128)}, f32[64,512]{1,0:T(8,128)}, f32[1,512]{1,0:T(1,128)}) custom-call(bf16[128,1024]{1,0:T(8,128)(2,1)} %copy-done.4, bf16[128,2048]{1,0:T(8,128)(2,1)} %copy-done.1, f32[64,1024]{1,0:T(8,128)} %copy-done.5, f32[64,512]{1,0:T(8,128)} %copy-done.6, ...), custom_call_target="tpu_custom_call" | custom-call | tf_op jit(solution)/shard_map/store_results/pallas_call | solution.py:565
Async XLA Ops:
  0.6 0.7 %copy-start.9 = (f32[512]{0:T(512)S(1)}, f32[512]{0:T(512)}, u32[]{:S(2)}) copy-start(f32[512]{0:T(512)} %param.11) | copy-start | bytes 6148
  0.6 0.7 %copy-start.10 = (s32[128]{0:T(128)S(1)}, s32[128]{0:T(128)}, u32[]{:S(2)}) copy-start(s32[128]{0:T(128)} %param.8) | copy-start | bytes 1540
  0.7 0.7 %copy-start.11 = (s32[1,4]{1,0:T(1,128)S(1)}, s32[1,4]{1,0:T(1,128)}, u32[]{:S(2)}) copy-start(s32[1,4]{1,0:T(1,128)} %len_in.1) | copy-start | bytes 52
  1.3 1.2 %copy-start = (bf16[512,1024]{1,0:T(8,128)(2,1)S(1)}, bf16[512,1024]{1,0:T(8,128)(2,1)}, u32[]{:S(2)}) copy-start(bf16[512,1024]{1,0:T(8,128)(2,1)} %wout_in.1) | copy-start | bytes 3145732
  2.5 1.0 %copy-start.2 = (bf16[128,2048]{1,0:T(8,128)(2,1)S(1)}, bf16[128,2048]{1,0:T(8,128)(2,1)}, u32[]{:S(2)}) copy-start(bf16[128,2048]{1,0:T(8,128)(2,1)} %qkvu_in.1) | copy-start | bytes 1572868
  3.6 0.9 %copy-start.3 = (bf16[128,1024]{1,0:T(8,128)(2,1)S(1)}, bf16[128,1024]{1,0:T(8,128)(2,1)}, u32[]{:S(2)}) copy-start(bf16[128,1024]{1,0:T(8,128)(2,1)} %cot_in.1) | copy-start | bytes 786436
  4.5 0.8 %copy-start.7 = (bf16[64,512]{1,0:T(8,128)(2,1)S(1)}, bf16[64,512]{1,0:T(8,128)(2,1)}, u32[]{:S(2)}) copy-start(bf16[64,512]{1,0:T(8,128)(2,1)} %table_in.1) | copy-start | bytes 196612
  42.3 0.8 %copy-start.1 = (bf16[128,2048]{1,0:T(8,128)(2,1)}, bf16[128,2048]{1,0:T(8,128)(2,1)S(1)}, u32[]{:S(2)}) copy-start(bf16[128,2048]{1,0:T(8,128)(2,1)S(1)} %get-tuple-element.16.refs_1_) | copy-start | bytes 1572868
  43.1 0.7 %copy-start.4 = (bf16[128,1024]{1,0:T(8,128)(2,1)}, bf16[128,1024]{1,0:T(8,128)(2,1)S(1)}, u32[]{:S(2)}) copy-start(bf16[128,1024]{1,0:T(8,128)(2,1)S(1)} %get-tuple-element.15.refs_0_) | copy-start | bytes 786436
  43.8 0.7 %copy-start.5 = (f32[64,1024]{1,0:T(8,128)}, f32[64,1024]{1,0:T(8,128)S(1)}, u32[]{:S(2)}) copy-start(f32[64,1024]{1,0:T(8,128)S(1)} %get-tuple-element.17.refs_2_) | copy-start | bytes 786436
  44.5 0.6 %copy-start.6 = (f32[64,512]{1,0:T(8,128)}, f32[64,512]{1,0:T(8,128)S(1)}, u32[]{:S(2)}) copy-start(f32[64,512]{1,0:T(8,128)S(1)} %get-tuple-element.18.refs_3_) | copy-start | bytes 393220
  45.2 0.6 %copy-start.8 = (f32[1,512]{1,0:T(1,128)}, f32[1,512]{1,0:T(1,128)S(1)}, u32[]{:S(2)}) copy-start(f32[1,512]{1,0:T(1,128)S(1)} %get-tuple-element.19.refs_4_) | copy-start | bytes 6148

commit v3 on v2

--- a/solution.py
+++ b/solution.py
@@ -555,7 +555,7 @@
             pltpu.SemaphoreType.DMA((10,)),
         ],
         compiler_params=pltpu.CompilerParams(
-            collective_id=0, has_side_effects=True, vmem_limit_bytes=48 * 1024 * 1024
+            collective_id=0, has_side_effects=True, vmem_limit_bytes=64 * 1024 * 1024
         ),
         name="attention_layer",
     )(
@@ -565,9 +565,10 @@
     output, d_qkvu, d_wout, d_table, d_gain = pl.pallas_call(
         store_kernel,
         out_shape=[jax.ShapeDtypeStruct(o.shape, o.dtype) for o in outs],
-        in_specs=[vmem] * 5,
+        in_specs=[pl.BlockSpec(memory_space=pl.ANY)] * 5,
         out_specs=[pl.BlockSpec(memory_space=pl.ANY)] * 5,
         scratch_shapes=[pltpu.SemaphoreType.DMA((5,))],
+        compiler_params=pltpu.CompilerParams(vmem_limit_bytes=64 * 1024 * 1024),
         name="store_results",
     )(*outs)
     return output, d_qkvu, d_wout, d_table, d_gain.reshape(width)

time: 48.7 us -> 76.1 us (1.56)
  Pallas kernels: 39.2 us -> 75 us
  local copies, waits for them, and re-layouts: 8.16 us -> 0 us
    pallas_call x1, Pallas kernels: 2.27 us -> 36.9 us  [on_device(): pl.pallas_call(store_kernel, out_shape=[jax.ShapeDtypeStruct(o.shape, o.d...]
    unnamed x24 -> x0, local copies, waits for them, and re-layouts: 8.16 us -> none
    pallas_call x1, Pallas kernels: 36.9 us -> 38 us  [on_device(): pl.pallas_call(functools.partial(layer_kernel, n_ctx, n_dp, f_parts), out...]
where the time goes in v3:
time: 76.1 us; the launch traced here: 75.6 us
  Pallas kernels  75 us (99%)
    pallas_call x1, Pallas kernels, on_device(): pl.pallas_call(functools.partial(layer_kernel, n_ctx, n_dp, f_parts), out...  38 us
    pallas_call x1, Pallas kernels, on_device(): pl.pallas_call(store_kernel, out_shape=[jax.ShapeDtypeStruct(o.shape, o.d...  36.9 us

profile of v3, /device:TPU:0, one launch (start us, length us, event | category | flops | bytes accessed | tf_op | source)
XLA Modules:
  0.0 75.6 jit_solution(13989304455286272346)
XLA Ops:
  0.6 38.0 %attention_layer.1 = (bf16[128,1024]{1,0:T(8,128)(2,1)}, bf16[128,2048]{1,0:T(8,128)(2,1)}, f32[64,1024]{1,0:T(8,128)}, f32[64,512]{1,0:T(8,128)}, f32[1,512]{1,0:T(1,128)}) custom-call(bf16[128,2048]{1,0:T(8,128)(2,1)} %qkvu_in.1, s32[1,128]{1,0:T(1,128)} %bitcast.4, s32[1,4]{1,0:T(1,128)} %len_in.1, bf16[64,512]{1,0:T(8,128)(2,1)} %table_in.1, ...), custom_call_target="tpu_custom_call" | custom-call | tf_op jit(solution)/shard_map/attention_layer/pallas_call | solution.py:506
  38.7 36.9 %store_results.1 = (bf16[128,1024]{1,0:T(8,128)(2,1)}, bf16[128,2048]{1,0:T(8,128)(2,1)}, f32[64,1024]{1,0:T(8,128)}, f32[64,512]{1,0:T(8,128)}, f32[1,512]{1,0:T(1,128)}) custom-call(bf16[128,1024]{1,0:T(8,128)(2,1)} %get-tuple-element.15.refs_0_, bf16[128,2048]{1,0:T(8,128)(2,1)} %get-tuple-element.16.refs_1_, f32[64,1024]{1,0:T(8,128)} %get-tuple-element.17.refs_2_, ...), custom_call_target="tpu_custom_call" | custom-call | tf_op jit(solution)/shard_map/store_results/pallas_call | solution.py:565

commit v4 on v3

--- a/solution.py
+++ b/solution.py
@@ -565,7 +565,7 @@
     output, d_qkvu, d_wout, d_table, d_gain = pl.pallas_call(
         store_kernel,
         out_shape=[jax.ShapeDtypeStruct(o.shape, o.dtype) for o in outs],
-        in_specs=[pl.BlockSpec(memory_space=pl.ANY)] * 5,
+        in_specs=[vmem] * 5,
         out_specs=[pl.BlockSpec(memory_space=pl.ANY)] * 5,
         scratch_shapes=[pltpu.SemaphoreType.DMA((5,))],
         compiler_params=pltpu.CompilerParams(vmem_limit_bytes=64 * 1024 * 1024),

time: 76.1 us -> 41.5 us (0.55)
  Pallas kernels: 75 us -> 40.3 us
    pallas_call x1, Pallas kernels: 36.9 us -> 2.27 us  [on_device(): pl.pallas_call(store_kernel, out_shape=[jax.ShapeDtypeStruct(o.shape, o.d...]
where the time goes in v4:
time: 41.5 us; the launch traced here: 40.9 us
  Pallas kernels  40.3 us (97%)
  between operations  0.64 us (2%)
    pallas_call x1, Pallas kernels, on_device(): pl.pallas_call(functools.partial(layer_kernel, n_ctx, n_dp, f_parts), out...  38 us
    pallas_call x1, Pallas kernels, on_device(): pl.pallas_call(store_kernel, out_shape=[jax.ShapeDtypeStruct(o.shape, o.d...  2.27 us

profile of v4, /device:TPU:0, one launch (start us, length us, event | category | flops | bytes accessed | tf_op | source)
XLA Modules:
  0.0 40.9 jit_solution(7729000211081016050)
XLA Ops:
  0.6 38.0 %attention_layer.1 = (bf16[128,1024]{1,0:T(8,128)(2,1)}, bf16[128,2048]{1,0:T(8,128)(2,1)}, f32[64,1024]{1,0:T(8,128)}, f32[64,512]{1,0:T(8,128)}, f32[1,512]{1,0:T(1,128)}) custom-call(bf16[128,2048]{1,0:T(8,128)(2,1)} %qkvu_in.1, s32[1,128]{1,0:T(1,128)} %bitcast.4, s32[1,4]{1,0:T(1,128)} %len_in.1, bf16[64,512]{1,0:T(8,128)(2,1)} %table_in.1, ...), custom_call_target="tpu_custom_call" | custom-call | tf_op jit(solution)/shard_map/attention_layer/pallas_call | solution.py:506
  38.7 2.3 %store_results.1 = (bf16[128,1024]{1,0:T(8,128)(2,1)}, bf16[128,2048]{1,0:T(8,128)(2,1)}, f32[64,1024]{1,0:T(8,128)}, f32[64,512]{1,0:T(8,128)}, f32[1,512]{1,0:T(1,128)}) custom-call(bf16[128,1024]{1,0:T(8,128)(2,1)} %get-tuple-element.15.refs_0_, bf16[128,2048]{1,0:T(8,128)(2,1)} %get-tuple-element.16.refs_1_, f32[64,1024]{1,0:T(8,128)} %get-tuple-element.17.refs_2_, ...), custom_call_target="tpu_custom_call" | custom-call | tf_op jit(solution)/shard_map/store_results/pallas_call | solution.py:565

commit v5 on v4

--- a/solution.py
+++ b/solution.py
@@ -200,24 +200,24 @@
         return dp_copy("gdp", gdp_src, gdp_buf.at[dpi], peer)
 
     def for_higher(action):
-        @pl.when(core == 0)
-        def _():
-            action(sibling)
-
         for d in range(1, chips):
             @pl.when(chip + d < chips)
             def _():
                 action(me + 2 * d)
 
-    def for_lower(action):
-        @pl.when(core == 1)
+        @pl.when(core == 0)
         def _():
             action(sibling)
 
+    def for_lower(action):
         for d in range(1, chips):
             @pl.when(chip >= d)
             def _():
                 action(me - 2 * d)
+
+        @pl.when(core == 1)
+        def _():
+            action(sibling)
 
     def for_partners(action):
         for d in range(1, chips):
@@ -350,6 +350,23 @@
     tab_buf[me] = tab_src[me]
     relay("q", q_buf, chip + 1, chips)
 
+    def project():
+        for_others(lambda p: ctx_arrived("cot", cot_buf, p))
+        ctx_arrived("mix", mix_buf, sibling)
+        for d in range(1, chips):
+            ctx_arrived("mix", mix_buf, lax.rem(sibling + 2 * d, n_ctx))
+        w_sum = dot_tn(
+            mix_buf[...].reshape(n_ctx * rows, width), cot_buf[...].reshape(n_ctx * rows, c_width)
+        )
+        wdp_src[...] = w_sum.astype(wdp_src.dtype)
+        for_dp_others(lambda p: wdp_copy(p).start())
+        own_rows = pl.multiple_of(dpi * dp_rows + part * p_rows, p_rows)
+        wdp_buf[dpi] = wdp_src[pl.ds(own_rows, p_rows)]
+
+    @pl.when(chip == chips - 1)
+    def _():
+        project()
+
     out_ref[...] = dot_nn(mixed, wout_ref[...]).astype(BF16)
 
     acc[...] = jnp.zeros_like(acc)
@@ -384,6 +401,10 @@
     lax.fori_loop(chip + 1, chips, key_side_direct, 0)
     lax.fori_loop(chip + 1, chips, key_side_relayed, 0)
     relay("mix", mix_buf, chip + 1, chips)
+
+    @pl.when(chip < chips - 1)
+    def _():
+        project()
 
     for_others(lambda p: ctx_arrived("gain", gain_buf, p))
     gain_sum = gain_buf[0]
@@ -399,18 +420,6 @@
     tdp_src[...] = tab_sum.astype(tdp_src.dtype)
     for_dp_others(lambda p: tdp_copy(p).start())
     tdp_buf[dpi] = tab_sum.astype(tdp_src.dtype)
-
-    for_others(lambda p: ctx_arrived("cot", cot_buf, p))
-    ctx_arrived("mix", mix_buf, sibling)
-    for d in range(1, chips):
-        ctx_arrived("mix", mix_buf, lax.rem(sibling + 2 * d, n_ctx))
-    w_sum = dot_tn(
-        mix_buf[...].reshape(n_ctx * rows, width), cot_buf[...].reshape(n_ctx * rows, c_width)
-    )
-    wdp_src[...] = w_sum.astype(wdp_src.dtype)
-    for_dp_others(lambda p: wdp_copy(p).start())
-    own_rows = pl.multiple_of(dpi * dp_rows + part * p_rows, p_rows)
-    wdp_buf[dpi] = wdp_src[pl.ds(own_rows, p_rows)]
 
     acc_k[...] = jnp.zeros_like(acc_k)
     acc_v[...] = jnp.zeros_like(acc_v)

time: 41.5 us -> 41.1 us (level); the launches traced: 40.9 us -> 41 us
  no operation moved by 1% of the time
where the time goes in v5:
time: 41.1 us; the launch traced here: 41 us
  Pallas kernels  40.3 us (98%)
  between operations  0.64 us (2%)
    pallas_call x1, Pallas kernels, on_device(): pl.pallas_call(functools.partial(layer_kernel, n_ctx, n_dp, f_parts), out...  38.1 us
    pallas_call x1, Pallas kernels, on_device(): pl.pallas_call(store_kernel, out_shape=[jax.ShapeDtypeStruct(o.shape, o.d...  2.27 us

profile of v5, /device:TPU:0, one launch (start us, length us, event | category | flops | bytes accessed | tf_op | source)
XLA Modules:
  0.0 41.0 jit_solution(15584911264295786966)
XLA Ops:
  0.6 38.1 %attention_layer.1 = (bf16[128,1024]{1,0:T(8,128)(2,1)}, bf16[128,2048]{1,0:T(8,128)(2,1)}, f32[64,1024]{1,0:T(8,128)}, f32[64,512]{1,0:T(8,128)}, f32[1,512]{1,0:T(1,128)}) custom-call(bf16[128,2048]{1,0:T(8,128)(2,1)} %qkvu_in.1, s32[1,128]{1,0:T(1,128)} %bitcast.4, s32[1,4]{1,0:T(1,128)} %len_in.1, bf16[64,512]{1,0:T(8,128)(2,1)} %table_in.1, ...), custom_call_target="tpu_custom_call" | custom-call | tf_op jit(solution)/shard_map/attention_layer/pallas_call | solution.py:515
  38.7 2.3 %store_results.1 = (bf16[128,1024]{1,0:T(8,128)(2,1)}, bf16[128,2048]{1,0:T(8,128)(2,1)}, f32[64,1024]{1,0:T(8,128)}, f32[64,512]{1,0:T(8,128)}, f32[1,512]{1,0:T(1,128)}) custom-call(bf16[128,1024]{1,0:T(8,128)(2,1)} %get-tuple-element.15.refs_0_, bf16[128,2048]{1,0:T(8,128)(2,1)} %get-tuple-element.16.refs_1_, f32[64,1024]{1,0:T(8,128)} %get-tuple-element.17.refs_2_, ...), custom_call_target="tpu_custom_call" | custom-call | tf_op jit(solution)/shard_map/store_results/pallas_call | solution.py:574
